TPU v7x, 256 devices: a whole 4x4x8 slice. The times are simulated.
256 devices in a mesh: depth: 8 (over y, z_lo), plane: 32 (over x, z_hi, core).
Axes of the slice: x: 4, y: 4, z: 8 (z_hi: 4, z_lo: 2; z = z_hi * 2 + z_lo), core: 2. Of those that a mesh axis runs over, the one named last changes fastest.
Arguments:
- velocity: float32 [24, 2048, 2048], P('depth', 'plane'), may hold values from 1.5 to 6
- dual_field: float32 [3, 24, 2048, 2048], P(None, 'depth', 'plane'), may hold values from -3 to 3
- kernel: float32 [24, 2048, 2048], P('depth', 'plane'), may hold values from 0.5 to 5
- data_spec: float32 [2048, 2048], P('plane'), may hold values from -12 to 12
Outputs:
- velocity_new: float32 [24, 2048, 2048], P('depth', 'plane')
- dual_new: float32 [3, 24, 2048, 2048], P(None, 'depth', 'plane')
All inputs are finite; a program needn't handle non-finite values.
Results may differ from a plain program's by a relative error of at most 0.0003.
Values sent between devices are 32-bit elements; how exact they have to be, the bound alone decides.
A program may use at most 128 MiB of HBM per device.

v0:
```python
import math

import jax
import jax.numpy as jnp
from jax import lax
from jax.sharding import PartitionSpec as P

gardner_coef = 1.741
dual_step = 0.25
primal_step = 0.25
tv_weight = 1.5
speed_floor = 1.5
speed_ceiling = 6.0
highest = lax.Precision.HIGHEST


def passed_along(block, axis, distance):
    devices = range(lax.axis_size(axis))
    route = [(i - distance, i) for i in devices if i - distance in devices]
    return lax.ppermute(block, axis, route)


def cas_matrix(length):
    counter = jnp.arange(length, dtype=jnp.int32)
    product = counter[:, None] * counter[None, :] % length
    angles = product.astype(jnp.float32) * (2.0 * math.pi / length)
    return (jnp.cos(angles) + jnp.sin(angles)) / math.sqrt(length)


def backward_diff(values, before, direction):
    trimmed = lax.slice_in_dim(values, 0, values.shape[direction] - 1, axis=direction)
    return values - jnp.concatenate([before, trimmed], axis=direction)


def project(candidates):
    magnitude = jnp.sqrt(jnp.sum(candidates * candidates, axis=0))
    return candidates / jnp.maximum(1.0, magnitude / tv_weight)


def body(velocity, dual_field, kernel, data_spec):
    planes = lax.axis_size("plane")
    depths = lax.axis_size("depth")
    plane_index = lax.axis_index("plane")
    depth_index = lax.axis_index("depth")
    layer_count, row_count, grid_size = velocity.shape
    col_count = grid_size // planes
    matrix = cas_matrix(grid_size)
    density = gardner_coef * jnp.power(velocity, 0.25)
    outgoing = jnp.einsum(
        "lrc,cbv->lbvr", density, matrix.reshape(grid_size, planes, col_count), precision=highest
    )
    outgoing = outgoing.reshape(layer_count, planes, col_count * row_count)
    received = lax.all_to_all(outgoing, "plane", split_axis=1, concat_axis=1, tiled=True)
    blocks = received.reshape(received.shape[0], planes, col_count, row_count)
    spectra = jnp.einsum(
        "lbvr,bru->lvu", blocks, matrix.reshape(planes, row_count, grid_size), precision=highest
    )
    partial_value = jnp.sum(kernel * spectra, axis=0)
    freq_col = plane_index * col_count + jnp.arange(col_count, dtype=jnp.int32)[:, None]
    summed = lax.psum(partial_value, "depth")
    freq_row = jnp.arange(grid_size, dtype=jnp.int32)[None, :]
    misfit = jnp.where((freq_col == 0) & (freq_row == 0), 0.0, summed - data_spec)
    weighted = kernel * misfit[None]
    returning = jnp.einsum(
        "lvu,ubr->lbvr", weighted, matrix.reshape(grid_size, planes, row_count), precision=highest
    )
    returning = returning.reshape(layer_count, planes, col_count * row_count)
    received = lax.all_to_all(returning, "plane", split_axis=1, concat_axis=1, tiled=True)
    blocks = received.reshape(received.shape[0], planes, col_count, row_count)
    adjoint = jnp.einsum(
        "lbvr,bvc->lrc", blocks, matrix.reshape(planes, col_count, grid_size), precision=highest
    )
    data_grad = 0.25 * density / velocity * adjoint
    total_layers = layer_count * depths
    col_ids = jnp.arange(grid_size, dtype=jnp.int32)[None, None, :]
    col_zeros = jnp.zeros((layer_count, row_count, 1), jnp.float32)
    layer_ids = depth_index * layer_count + jnp.arange(layer_count, dtype=jnp.int32)[:, None, None]
    row_ids = plane_index * row_count + jnp.arange(row_count, dtype=jnp.int32)[None, :, None]
    next_rows = passed_along(velocity[:, :1, :], "plane", -1)
    next_layer = passed_along(velocity[:1], "depth", -1)
    diff_rows = jnp.concatenate([velocity[:, 1:], next_rows], axis=1) - velocity
    diff_cols = jnp.concatenate([velocity[:, :, 1:], velocity[:, :, -1:]], axis=2) - velocity
    diff_layers = jnp.concatenate([velocity[1:], next_layer], axis=0) - velocity
    q_rows = jnp.where(row_ids < grid_size - 1, dual_field[0] + dual_step * diff_rows, 0.0)
    q_cols = jnp.where(col_ids < grid_size - 1, dual_field[1] + dual_step * diff_cols, 0.0)
    q_layers = jnp.where(layer_ids < total_layers - 1, dual_field[2] + dual_step * diff_layers, 0.0)
    dual_new = project(jnp.stack([q_rows, q_cols, q_layers]))
    prev_rows = passed_along(dual_new[0][:, -1:, :], "plane", 1)
    prev_layer = passed_along(dual_new[2][-1:], "depth", 1)
    divergence = (
        backward_diff(dual_new[0], prev_rows, 1)
        + backward_diff(dual_new[1], col_zeros, 2)
        + backward_diff(dual_new[2], prev_layer, 0)
    )
    update = velocity - primal_step * (data_grad - divergence)
    return (jnp.clip(update, speed_floor, speed_ceiling), dual_new)


def solution(mesh):
    in_specs = (
        P("depth", "plane", None),
        P(None, "depth", "plane", None),
        P("depth", "plane", None),
        P("plane", None),
    )
    out_specs = (P("depth", "plane", None), P(None, "depth", "plane", None))
    return jax.shard_map(body, mesh=mesh, in_specs=in_specs, out_specs=out_specs, check_vma=False)
```

profile of v0, /device:TPU:6, one launch (start us, length us, event | category | flops | bytes accessed | tf_op | source)
XLA Modules:
  0.0 571.2 jit_solution(18106866664365786167)
XLA Ops:
  7.2 2.0 fusion.115
  9.1 95.3 %fusion.33 = f32[3,32,64,64]{3,2,0,1:T(8,128)} fusion(s32[32,64]{1,0:T(8,128)S(1)} %multiply_add_fusion, f32[3,64,2048,1]{2,1,0,3:T(8,128)S(1)} %fusion.115), kind=kOutput, calls=%fused_computation.35 | convolution fusion | flops 9730785280 | bytes 3153920 | tf_op jit(solution)/shard_map/lrc,cbv->lbvr/dot_general | solution.py:49
  104.4 0.0 copy-start
  104.4 4.9 reshape.162
  109.3 11.7 %all-to-all-start = ((f32[3,32,4096]{2,0,1:T(4,128)}), f32[3,32,4096]{2,0,1:T(4,128)}, u32[]{:S(2)}, u32[]{:S(2)}) async-start(f32[3,32,4096]{2,0,1:T(4,128)} %reshape.162), calls=%async_computation | async-start | bytes 4194304 | tf_op jit(solution)/shard_map/all_to_all | solution.py:53
  120.9 0.0 all-reduce.3.cloned.1.call-start
  121.0 0.0 copy-done
  121.0 5.5 collective-permute-start
  126.5 0.8 slice.69
  127.3 1.3 collective-permute-start.1
  128.6 1.3 slice.62
  129.9 0.1 slice.66
  130.0 1.6 slice.65
  131.7 69.9 %fusion.119 = f32[32,64,2048,1]{2,1,0,3:T(8,128)} fusion(s32[32,64]{1,0:T(8,128)S(1)} %multiply_add_fusion), kind=kLoop, calls=%fused_computation.15.clone.clone.clone.clone.clone.clone.clone.1 | loop fusion | flops 67108864 | bytes 16785408 | tf_op jit(solution)/shard_map/lbvr,bru->lvu/dot_general | solution.py:55
  201.6 0.0 copy-start.4
  201.6 0.0 all-to-all-done
  201.6 2.6 copy.11
  204.2 2.4 reshape.153
  206.6 0.0 copy-done.4
  206.6 0.0 copy-start.5
  206.6 17.1 %fusion.65 = f32[64,2048]{1,0:T(8,128)} fusion(f32[3,64,2048]{2,1,0:T(8,128)S(1)} %copy-done.4, f32[3,32,64,64]{3,2,1,0:T(8,128)} %reshape.153, f32[32,64,2048,1]{2,1,0,3:T(8,128)} %fusion.119), kind=kOutput, calls=%fused_computation.69 | convolution fusion | flops 9664331776 | bytes 20447232 | tf_op jit(solution)/shard_map/lbvr,bru->lvu/dot_general | solution.py:55
  223.7 0.0 all-reduce.3.cloned.1.call-update
  223.8 80.0 %all-reduce.3.cloned.1.call-done = f32[64,2048]{1,0:T(8,128)} async-done(((f32[64,2048]{1,0:T(8,128)}), f32[64,2048]{1,0:T(8,128)}) %all-reduce.3.cloned.1.call-update) | async-done | bytes 524304 | tf_op jit(solution)/shard_map/psum | solution.py:60
  303.8 0.0 copy-done.5
  303.8 1.2 subtract_select_fusion
  305.0 0.2 fusion.117
  305.2 95.1 %fusion.36 = f32[3,32,64,64]{2,3,0,1:T(8,128)S(1)} fusion(s32[32,64]{1,0:T(8,128)S(1)} %multiply_add_fusion, f32[3,64,2048,1]{2,1,0,3:T(8,128)S(1)} %fusion.117), kind=kOutput, calls=%fused_computation.36 | convolution fusion | flops 9730785280 | bytes 3153920 | tf_op jit(solution)/shard_map/lvu,ubr->lbvr/dot_general | solution.py:64
  400.2 2.5 copy.21
  402.8 0.0 copy-start.1
  402.8 0.0 slice-start
  402.8 4.7 reshape.163
  407.5 9.3 %all-to-all-start.1 = ((f32[3,32,4096]{2,0,1:T(4,128)}), f32[3,32,4096]{2,0,1:T(4,128)}, u32[]{:S(2)}, u32[]{:S(2)}) async-start(f32[3,32,4096]{2,0,1:T(4,128)} %reshape.163), calls=%async_computation.1 | async-start | bytes 4194304 | tf_op jit(solution)/shard_map/all_to_all | solution.py:68
  416.9 0.0 collective-permute-done
  416.9 0.0 collective-permute-done.1
  416.9 0.0 copy-done.1
  416.9 0.0 slice-done
  416.9 4.7 fusion.48
  421.6 0.6 multiply_reduce_fusion
  422.2 0.5 multiply_maximum_fusion
  422.7 0.7 fusion.20
  423.4 0.0 copy-start.2
  423.5 2.6 collective-permute-start.3
  426.1 1.5 slice_bitcast_fusion.1
  427.6 0.0 copy-start.3
  427.6 1.2 copy-done.3
  428.8 1.9 collective-permute-start.2
  430.7 0.0 copy-done.2
  430.7 0.1 slice_bitcast_fusion.3
  430.8 36.1 %all-to-all-done.1 = f32[3,32,4096]{2,0,1:T(4,128)} async-done(((f32[3,32,4096]{2,0,1:T(4,128)}), f32[3,32,4096]{2,0,1:T(4,128)}, u32[]{:S(2)}, u32[]{:S(2)}) %all-to-all-start.1) | async-done | bytes 1572896 | tf_op jit(solution)/shard_map/all_to_all | solution.py:68
  466.8 4.6 reshape.164
  471.5 6.9 %collective-permute-done.2 = f32[3,1,2048]{2,1,0:T(1,128)S(1)} collective-permute-done((f32[3,1,2048]{2,1,0:T(1,128)S(1)}, f32[3,1,2048]{2,1,0:T(1,128)S(1)}, u32[]{:S(2)}, u32[]{:S(2)}) %collective-permute-start.2) | collective-permute-done | bytes 24608 | tf_op jit(solution)/shard_map/ppermute | solution.py:20
  478.4 0.0 collective-permute-done.3
  478.4 85.8 %fusion.44 = f32[3,64,2048]{2,1,0:T(8,128)} fusion(f32[3,64,2048]{2,1,0:T(8,128)S(1)} %copy-done.1, f32[3,3,64,2048]{3,2,1,0:T(8,128)} %copy-done.2, f32[3,63,2048]{2,1,0:T(8,128)} %bitcast.142, f32[3,1,2048]{2,1,0:T(1,128)S(1)} %collective-permute-done.2, f32[2,64,2048]{2,1,0:T(8,128)S(1)} %slice_bitcast_fusion.3, ...), kind=kOutput, calls=%fused_computation.43 | convolution fusion | flops 9736290304 | bytes 14163200 | tf_op jit(solution)/shard_map/lbvr,bvc->lrc/dot_general | solution.py:70
  (9 shorter events, 0.1 us)
Async XLA Ops:
  104.4 16.6 %copy-start = (f32[3,64,2048]{2,1,0:T(8,128)S(1)}, f32[3,64,2048]{2,1,0:T(8,128)}, u32[]{:S(2)}) copy-start(f32[3,64,2048]{2,1,0:T(8,128)} %param.4) | copy-start | bytes 4718596
  109.3 92.3 %all-to-all-start = ((f32[3,32,4096]{2,0,1:T(4,128)}), f32[3,32,4096]{2,0,1:T(4,128)}, u32[]{:S(2)}, u32[]{:S(2)}) async-start(f32[3,32,4096]{2,0,1:T(4,128)} %reshape.162), calls=%async_computation | async-start | bytes 4194304 | tf_op jit(solution)/shard_map/all_to_all | solution.py:53
  120.9 182.9 %all-reduce.3.cloned.1.call-start = ((), (), s32[]{:S(2)}) async-start(), calls=%async_computation.2 | async-start | bytes 1048576 | tf_op jit(solution)/shard_map/psum | solution.py:60
  121.0 295.9 %collective-permute-start = (f32[3,1,2048]{2,1,0:T(1,128)S(1)}, f32[3,1,2048]{2,1,0:T(1,128)S(1)}, u32[]{:S(2)}, u32[]{:S(2)}) collective-permute-start(f32[3,1,2048]{2,1,0:T(1,128)S(1)} %slice.63), channel_id=1, source_target_pairs={{1,0},{2,1},{3,2},{4,3},{5,4},{6,5},{7,6},{8,7},{9,8},{10,9},{11,1... | collective-permute-start | bytes 73736 | tf_op jit(solution)/shard_map/ppermute | solution.py:20
  127.3 289.5 %collective-permute-start.1 = (f32[1,64,2048]{2,1,0:T(8,128)}, f32[1,64,2048]{2,1,0:T(8,128)}, u32[]{:S(2)}, u32[]{:S(2)}) collective-permute-start(f32[1,64,2048]{2,1,0:T(8,128)} %slice.69), channel_id=1, source_target_pairs={{32,0},{64,32},{96,64},{128,96},{160,128},{192,160},{224,192},{33,... | collective-permute-start | bytes 1572872 | tf_op jit(solution)/shard_map/ppermute | solution.py:20
  201.6 5.1 copy-start.4
  206.6 97.2 %copy-start.5 = (f32[64,2048]{1,0:T(8,128)S(1)}, f32[64,2048]{1,0:T(8,128)}, u32[]{:S(2)}) copy-start(f32[64,2048]{1,0:T(8,128)} %param.7) | copy-start | bytes 1572868
  402.8 14.1 %copy-start.1 = (f32[3,64,2048]{2,1,0:T(8,128)S(1)}, f32[3,64,2048]{2,1,0:T(8,128)}, u32[]{:S(2)}) copy-start(f32[3,64,2048]{2,1,0:T(8,128)} %param.4) | copy-start | bytes 4718596
  402.8 14.1 %slice-start = ((f32[3,64,2048]{2,1,0:T(8,128)}), f32[2,64,2048]{2,1,0:T(8,128)S(1)}, s32[]{:S(2)}) async-start(f32[3,64,2048]{2,1,0:T(8,128)} %param.4), calls=%async_computation.3 | async-start | bytes 2097152 | tf_op jit(solution)/shard_map/slice | solution.py:83
  407.5 59.3 %all-to-all-start.1 = ((f32[3,32,4096]{2,0,1:T(4,128)}), f32[3,32,4096]{2,0,1:T(4,128)}, u32[]{:S(2)}, u32[]{:S(2)}) async-start(f32[3,32,4096]{2,0,1:T(4,128)} %reshape.163), calls=%async_computation.1 | async-start | bytes 4194304 | tf_op jit(solution)/shard_map/all_to_all | solution.py:68
  423.4 7.3 %copy-start.2 = (f32[3,3,64,2048]{3,2,1,0:T(8,128)}, f32[3,3,64,2048]{3,2,1,0:T(8,128)S(1)}, u32[]{:S(2)}) copy-start(f32[3,3,64,2048]{3,2,1,0:T(8,128)S(1)} %fusion.20) | copy-start | bytes 14155780
  423.5 54.9 %collective-permute-start.3 = (f32[1,64,2048]{2,1,0:T(8,128)S(1)}, f32[1,64,2048]{2,1,0:T(8,128)}, u32[]{:S(2)}, u32[]{:S(2)}) collective-permute-start(f32[1,64,2048]{2,1,0:T(8,128)S(1)} %slice_bitcast_fusion.4), channel_id=1, source_target_pairs={{0,32},{32,64},{64,96},{96,128},{128,160},{160,192},{192,224},{1,3... | collective-permute-start | bytes 1572872 | tf_op jit(solution)/shard_map/ppermute | solution.py:20
  427.6 1.2 copy-start.3
  428.8 49.6 %collective-permute-start.2 = (f32[3,1,2048]{2,1,0:T(1,128)S(1)}, f32[3,1,2048]{2,1,0:T(1,128)S(1)}, u32[]{:S(2)}, u32[]{:S(2)}) collective-permute-start(f32[3,1,2048]{2,1,0:T(1,128)S(1)} %slice.81), channel_id=1, source_target_pairs={{0,1},{1,2},{2,3},{3,4},{4,5},{5,6},{6,7},{7,8},{8,9},{9,10},{10,1... | collective-permute-start | bytes 73736 | tf_op jit(solution)/shard_map/ppermute | solution.py:20
Sparse Core Ops, SparseCore 0:
  223.9 79.9 all-reduce.2
where the time goes:
time: 581 us; the launch traced here: 571 us
  matrix products  293 us (50%)
  waiting for transfers between devices  123 us (21%)
  other arithmetic  79.7 us (14%)
  starting transfers between devices  32.4 us (6%)
  local copies, waits for them, and re-layouts  28.5 us (5%)
  between operations  14.4 us (2%)
    dot_general x1, matrix products, body(): jnp.einsum('lrc,cbv->lbvr', density, matrix.reshape(grid_size, planes, co...  95.3 us
    dot_general x1, matrix products, body(): jnp.einsum('lvu,ubr->lbvr', weighted, matrix.reshape(grid_size, planes, r...  95.1 us
    dot_general x1, matrix products, body(): jnp.einsum('lbvr,bvc->lrc', blocks, matrix.reshape(planes, col_count, gri...  85.8 us
    psum x1, waiting for transfers between devices, body(): summed = lax.psum(partial_value, 'depth')  80 us
    dot_general x1, other arithmetic, body(): jnp.einsum('lbvr,bru->lvu', blocks, matrix.reshape(planes, row_count, gri...  69.9 us
    all_to_all x1, waiting for transfers between devices, body(): lax.all_to_all(returning, 'plane', split_axis=1, concat_axis=1, tiled=True)  36.1 us
    dot_general x1, matrix products, body(): jnp.einsum('lbvr,bru->lvu', blocks, matrix.reshape(planes, row_count, gri...  17.1 us
    all_to_all x1, starting transfers between devices, body(): lax.all_to_all(outgoing, 'plane', split_axis=1, concat_axis=1, tiled=True)  11.7 us
  transfers between devices with their start and end apart: 7, of which 3 were waited for; matrix products, arithmetic and copies ran while one was open for 37% of the time, Pallas kernels for 0%

commit v1 on v0

v1 whole, which is shorter than its diff:
```python
import functools
import math

import jax
import jax.numpy as jnp
import ml_dtypes
import numpy as np
from jax import lax
from jax.experimental import pallas as pl
from jax.experimental.pallas import tpu as pltpu
from jax.sharding import PartitionSpec as P

gardner_coef = 1.741
dual_step = 0.25
primal_step = 0.25
tv_weight = 1.5
speed_floor = 1.5
speed_ceiling = 6.0
density_shift = 2.326
chunks = 2
block = 256
MESH = pl.DeviceIdType.MESH
f32, bf16 = jnp.float32, jnp.bfloat16


def cas_parts(length):
    counter = np.arange(length, dtype=np.int64)
    angles = (counter[:, None] * counter[None, :] % length) * (2.0 * math.pi / length)
    matrix = ((np.cos(angles) + np.sin(angles)) / math.sqrt(length)).astype(np.float32)
    high = matrix.astype(ml_dtypes.bfloat16)
    low = (matrix - high.astype(np.float32)).astype(ml_dtypes.bfloat16)
    return high, low


def split(values):
    high = values.astype(bf16)
    return high, (values - high.astype(f32)).astype(bf16)


def dot(left, right):
    return jnp.dot(left, right, preferred_element_type=f32)


def step_kernel(
    planes, depths, size, layers,
    vel_in, dual_in, kern_in, data_in, ahi_in, alo_in,
    vel_out, dual_out,
    vel, dual, kern, data, ahi, alo, dt0h, dt0l, dt1h, dt1l,
    gsend, grecv, bsend, brecv, lhs, part, rsum, rrecv, zrecv, misfit, xt, acc, base,
    hsend, hrecv, psend, precv, layer_next, layer_prev,
    in_sem, a_sem, out_sem, gs_sem, gr_sem, bs_sem, br_sem, rs_sem, rr_sem, z_sem, ms_sem, mr_sem, h_sem,
):
    rows = size // planes
    span = rows // chunks
    half = span // 2
    slots = 2 * chunks
    group = min(8, planes)
    ny = depths // 2
    quarter = span // ny
    blocks = size // block
    per_block = block // rows
    me = lax.axis_index("plane")
    my_depth = lax.axis_index("depth")
    y, z = my_depth // 2, my_depth % 2
    home, seat = me // group, me % group

    def target(t):
        return ((home + t // group) % (planes // group)) * group + (seat + t % group) % group

    def y_peer(i):
        return ((y + i) % ny) * 2 + z

    after, before = (me + 1) % planes, (me + planes - 1) % planes
    above, below = (my_depth + 1) % depths, (my_depth + depths - 1) % depths
    sibling = y * 2 + (1 - z)
    diagonal = jnp.where(z == 0, below, above)

    loads = [
        pltpu.make_async_copy(src, dst, in_sem.at[i])
        for i, (src, dst) in enumerate(
            [(vel_in, vel.at[:, pl.ds(0, rows), :]), (dual_in, dual), (kern_in, kern), (data_in, data)]
        )
    ]
    loads[0].start()
    a_loads = [
        (
            pltpu.make_async_copy(ahi_in.at[:, s], ahi.at[:, s], a_sem.at[0, s]),
            pltpu.make_async_copy(alo_in.at[:, s], alo.at[:, s], a_sem.at[1, s]),
        )
        for s in range(slots)
    ]
    for pair in a_loads[:2]:
        for copy in pair:
            copy.start()
    loads[1].start()
    for pair in a_loads[2:]:
        for copy in pair:
            copy.start()
    loads[2].start()
    loads[3].start()

    barrier = pltpu.get_barrier_semaphore()

    def greet(t, _):
        pl.semaphore_signal(barrier, inc=1, device_id={"plane": target(t)}, device_id_type=MESH)
        return 0

    lax.fori_loop(1, planes, greet, 0)
    for i in range(1, ny):
        pl.semaphore_signal(barrier, inc=1, device_id={"depth": y_peer(i)}, device_id_type=MESH)
    pl.semaphore_signal(barrier, inc=1, device_id={"depth": sibling}, device_id_type=MESH)
    pl.semaphore_signal(barrier, inc=1, device_id={"depth": diagonal}, device_id_type=MESH)

    lane = lax.broadcasted_iota(jnp.int32, (half, 128), 1)
    left = lane < 64

    def swap(values):
        return pltpu.roll(values, 64, 1)

    loads[0].wait()

    def transpose_density(i, _):
        off = pl.multiple_of(i * 128, 128)
        where = pl.ds(off, 128)
        d = [gardner_coef * jnp.sqrt(jnp.sqrt(vel[l, 0:rows, where])) - density_shift for l in range(layers)]
        pair = jnp.concatenate([d[0], d[1]], axis=0).T
        third = jnp.concatenate([d[2], jnp.zeros_like(d[2])], axis=0).T
        pair_h, pair_l = split(pair)
        third_h, third_l = split(third)
        other_h, other_l = split(swap(third))
        dt0h[where, 0:128] = pair_h
        dt0l[where, 0:128] = pair_l
        dt1h[where, 0:128] = pair_h
        dt1l[where, 0:128] = pair_l
        dt0h[where, 128:256] = third_h
        dt0l[where, 128:256] = third_l
        dt1h[where, 128:256] = other_h
        dt1l[where, 128:256] = other_l
        return 0

    lax.fori_loop(0, size // 128, transpose_density, 0)
    for l in range(layers):
        hsend[l : l + 1, :] = vel[l, 0:1, :]
    for l in range(layers, 8):
        hsend[l : l + 1, :] = jnp.zeros((1, size), f32)

    pl.semaphore_wait(barrier, planes + ny)

    row_copy = pltpu.make_async_remote_copy(
        src_ref=hsend, dst_ref=hrecv, send_sem=h_sem.at[0], recv_sem=h_sem.at[1],
        device_id={"plane": before}, device_id_type=MESH)
    row_copy.start()
    layer_copy = pltpu.make_async_remote_copy(
        src_ref=vel_in.at[0], dst_ref=layer_next, send_sem=h_sem.at[2], recv_sem=h_sem.at[3],
        device_id={"depth": below}, device_id_type=MESH)
    layer_copy.start()

    def g_copy(k, t, who):
        to = target(t)
        return pltpu.make_async_remote_copy(
            src_ref=gsend.at[k, to], dst_ref=grecv.at[k, who], send_sem=gs_sem.at[k, to], recv_sem=gr_sem.at[k, who],
            device_id={"plane": to}, device_id_type=MESH)

    def b_copy(k, t, who):
        to = target(t)
        return pltpu.make_async_remote_copy(
            src_ref=bsend.at[k, to], dst_ref=brecv.at[k, who], send_sem=bs_sem.at[k, to], recv_sem=br_sem.at[k, who],
            device_id={"plane": to}, device_id_type=MESH)

    def columns(k, send):
        def one(g, _):
            first = pl.multiple_of(((home + g) % (planes // group)) * group, group)
            there = pl.ds(first, group)
            outs = []
            for h, (high, low) in enumerate([(dt0h, dt0l), (dt1h, dt1l)]):
                a_h = ahi[there, 2 * k + h].reshape(group * half, size)
                a_l = alo[there, 2 * k + h].reshape(group * half, size)
                both = dot(jnp.concatenate([a_h, a_l], axis=0), high[...])
                outs.append(both[: group * half] + both[group * half :] + dot(a_h, low[...]))
            gsend[k, there, :, 0:128] = outs[0][:, 0:128].reshape(group, half, 128)
            gsend[k, there, :, 128:256] = outs[1][:, 0:128].reshape(group, half, 128)
            gsend[k, there, :, 256:384] = (outs[0][:, 128:256] + outs[1][:, 128:256]).reshape(group, half, 128)
            if send:
                def start(t, _):
                    g_copy(k, t, me).start()
                    return 0

                lax.fori_loop(jnp.maximum(g * group, 1), (g + 1) * group, start, 0)
            return 0

        lax.fori_loop(0, planes // group, one, 0)
        grecv[k, me] = gsend[k, me]

    for pair in a_loads[:2]:
        for copy in pair:
            copy.wait()
    columns(0, True)
    for pair in a_loads[2:]:
        for copy in pair:
            copy.wait()
    columns(1, False)

    row8 = lax.broadcasted_iota(jnp.int32, (8, size), 0)
    col8 = lax.broadcasted_iota(jnp.int32, (8, size), 1)
    loads[1].wait()
    row_copy.wait()
    layer_copy.wait()
    for l in range(layers):
        vel[l, rows : rows + 1, :] = hrecv[l : l + 1, :]

    for l in range(layers):
        def dual_rows(i, _, l=l):
            off = pl.multiple_of(i * 8, 8)
            here = pl.ds(off, 8)
            v = vel[l, here, :]
            following = vel[l, pl.ds(pl.multiple_of(off + 8, 8), 8), :][0:1]
            next_row = jnp.where(row8 == 7, following, pltpu.roll(v, 7, 0))
            next_col = pltpu.roll(v, size - 1, 1)
            next_layer = vel[l + 1, here, :] if l + 1 < layers else layer_next[here, :]
            last_row = (me * rows + off + row8) == size - 1
            q0 = jnp.where(last_row, 0.0, dual[0, l, here, :] + dual_step * (next_row - v))
            q1 = jnp.where(col8 == size - 1, 0.0, dual[1, l, here, :] + dual_step * (next_col - v))
            q2 = dual[2, l, here, :] + dual_step * (next_layer - v)
            if l + 1 == layers:
                q2 = jnp.where(my_depth == depths - 1, 0.0, q2)
            scale = lax.rsqrt(jnp.maximum(1.0, (q0 * q0 + q1 * q1 + q2 * q2) * (1.0 / (tv_weight * tv_weight))))
            dual[0, l, here, :] = q0 * scale
            dual[1, l, here, :] = q1 * scale
            dual[2, l, here, :] = q2 * scale
            return 0

        lax.fori_loop(0, rows // 8, dual_rows, 0)
    for l in range(layers):
        psend[l : l + 1, :] = dual[0, l, rows - 1 : rows, :]
    for l in range(layers, 8):
        psend[l : l + 1, :] = jnp.zeros((1, size), f32)
    dual_store = pltpu.make_async_copy(dual, dual_out, out_sem.at[0])
    dual_store.start()
    prow_copy = pltpu.make_async_remote_copy(
        src_ref=psend, dst_ref=precv, send_sem=h_sem.at[4], recv_sem=h_sem.at[5],
        device_id={"plane": after}, device_id_type=MESH)
    prow_copy.start()
    player_copy = pltpu.make_async_remote_copy(
        src_ref=dual.at[2, layers - 1], dst_ref=layer_prev, send_sem=h_sem.at[6], recv_sem=h_sem.at[7],
        device_id={"depth": above}, device_id_type=MESH)
    player_copy.start()

    def g_next(t, _):
        g_copy(0, t, me).wait_send()
        g_copy(1, t, me).start()
        return 0

    lax.fori_loop(1, planes, g_next, 0)
    loads[2].wait()
    loads[3].wait()

    def rows_in(k):
        def arrived(t, _):
            g_copy(k, t, target(t)).wait_recv()
            return 0

        lax.fori_loop(1, planes, arrived, 0)

        def assemble(m, _):
            even, odd = grecv[k, 2 * m], grecv[k, 2 * m + 1]
            a, b, c = (even[:, 0:128], odd[:, 0:128]), (even[:, 128:256], odd[:, 128:256]), (even[:, 256:384], odd[:, 256:384])
            first = lambda p: jnp.where(left, p[0], swap(p[1]))
            second = lambda p: jnp.where(left, swap(p[0]), p[1])
            whole = jnp.concatenate([first(a), first(b), second(a), second(b), first(c), second(c)], axis=0)
            high, low = split(whole)
            there = pl.ds(pl.multiple_of(m * 128, 128), 128)
            lhs[0 : layers * span, there] = high
            lhs[layers * span : 2 * layers * span, there] = low
            return 0

        lax.fori_loop(0, planes // 2, assemble, 0)

    def times_matrix(n):
        there = pl.ds(pl.multiple_of(n * block, block), block)
        a_h = ahi[:, :, :, there].reshape(size, block)
        a_l = alo[:, :, :, there].reshape(size, block)
        count = layers * span
        both = dot(lhs[...], a_h)
        return there, both[:count] + both[count:] + dot(lhs[0:count, :], a_l)

    def weigh(k):
        def one(n, _):
            there, spectra = times_matrix(n)
            weights = kern[:, k * span : (k + 1) * span, there]
            part[k, :, there] = jnp.sum(weights * spectra.reshape(layers, span, block), axis=0)
            return 0

        lax.fori_loop(0, blocks, one, 0)

    def r_copy(k, i):
        to = (y + i) % ny
        return pltpu.make_async_remote_copy(
            src_ref=part.at[k, pl.ds(pl.multiple_of(to * quarter, quarter), quarter)], dst_ref=rrecv.at[k, i],
            send_sem=rs_sem.at[k, i], recv_sem=rr_sem.at[k, i],
            device_id={"depth": y_peer(i)}, device_id_type=MESH)

    def z_copy(k):
        return pltpu.make_async_remote_copy(
            src_ref=rsum.at[k], dst_ref=zrecv.at[k], send_sem=z_sem.at[0, k], recv_sem=z_sem.at[1, k],
            device_id={"depth": sibling}, device_id_type=MESH)

    mine = pl.ds(pl.multiple_of(y * quarter, quarter), quarter)

    def m_copy(k, i):
        return pltpu.make_async_remote_copy(
            src_ref=misfit.at[k, mine], dst_ref=misfit.at[k, mine],
            send_sem=ms_sem.at[k, i], recv_sem=mr_sem.at[k, i],
            device_id={"depth": y_peer(i)}, device_id_type=MESH)

    def m_arrival(k, i):
        theirs = pl.ds(pl.multiple_of(((y + ny - i) % ny) * quarter, quarter), quarter)
        return pltpu.make_async_remote_copy(
            src_ref=misfit.at[k, mine], dst_ref=misfit.at[k, theirs],
            send_sem=ms_sem.at[k, i], recv_sem=mr_sem.at[k, i],
            device_id={"depth": y_peer(i)}, device_id_type=MESH)

    def reduce_rows(k):
        total = part[k, mine, :]
        for i in range(1, ny):
            r_copy(k, i).wait_recv()
            total = total + rrecv[k, i]
        rsum[k] = total
        z_copy(k).start()

    def spread(k):
        z_copy(k).wait_recv()
        first = k * span + y * quarter
        summed = rsum[k] + zrecv[k]
        values = summed - data[pl.ds(pl.multiple_of(first, quarter), quarter), :]
        freq_col = me * rows + first + lax.broadcasted_iota(jnp.int32, (quarter, size), 0)
        freq_row = lax.broadcasted_iota(jnp.int32, (quarter, size), 1)
        misfit[k, mine, :] = jnp.where((freq_col == 0) & (freq_row == 0), 0.0, values)
        for i in range(1, ny):
            m_copy(k, i).start()

    def rows_out(k):
        for i in range(1, ny):
            m_arrival(k, i).wait_recv()
        count = layers * span

        def load(n, _):
            there = pl.ds(pl.multiple_of(n * block, block), block)
            weighted = kern[:, k * span : (k + 1) * span, there] * misfit[k, :, there][None]
            high, low = split(weighted.reshape(count, block))
            lhs[0:count, there] = high
            lhs[count : 2 * count, there] = low
            return 0

        lax.fori_loop(0, blocks, load, 0)
        left_all = lax.broadcasted_iota(jnp.int32, (layers, half, 128), 2) < 64

        def one(i, _):
            n = (home * (group // per_block) + i) % blocks
            _, values = times_matrix(n)
            for s in range(block // 128):
                slab = values[:, s * 128 : (s + 1) * 128].reshape(layers, 2, half, 128)
                top, low = slab[:, 0], slab[:, 1]
                even = jnp.where(left_all, top, pltpu.roll(low, 64, 2))
                odd = jnp.where(left_all, pltpu.roll(top, 64, 2), low)
                bsend[k, n * per_block + 2 * s] = even.reshape(layers * half, 128)
                bsend[k, n * per_block + 2 * s + 1] = odd.reshape(layers * half, 128)

            @pl.when(i % (group // per_block) == group // per_block - 1)
            def _():
                g = i // (group // per_block)

                def start(t, _):
                    b_copy(k, t, me).start()
                    return 0

                lax.fori_loop(jnp.maximum(g * group, 1), (g + 1) * group, start, 0)

            return 0

        lax.fori_loop(0, blocks, one, 0)
        brecv[k, me] = bsend[k, me]

    def columns_back(k, last):
        def arrived(t, _):
            b_copy(k, t, target(t)).wait_recv()
            return 0

        lax.fori_loop(1, planes, arrived, 0)
        high_rows = layers * rows
        many = 128 // half

        for l in range(layers):
            def turn(i, _, l=l):
                who = pl.ds(pl.multiple_of(i * many, many), many)
                tile = brecv[k, who, l * half : (l + 1) * half, :].reshape(128, 128).T
                high, low = split(tile)
                for h in range(2):
                    there = pl.ds(pl.multiple_of(h * planes * half + i * 128, 128), 128)
                    xt[l * rows : (l + 1) * rows, there] = high[h * 64 : (h + 1) * 64]
                    xt[high_rows + l * rows : high_rows + (l + 1) * rows, there] = low[h * 64 : (h + 1) * 64]
                return 0

            lax.fori_loop(0, planes // many, turn, 0)

        def one(n, _):
            there = pl.ds(pl.multiple_of(n * block, block), block)
            total = acc[:, there] if last else None
            for h in range(2):
                a_h = ahi[:, 2 * k + h, :, there].reshape(planes * half, block)
                a_l = alo[:, 2 * k + h, :, there].reshape(planes * half, block)
                part_x = xt[:, h * planes * half : (h + 1) * planes * half]
                both = dot(part_x, a_h)
                new = both[:high_rows] + both[high_rows:] + dot(part_x[:high_rows], a_l)
                total = new if total is None else total + new
            if last:
                adjoint = total.reshape(layers, rows, block)
                update = base[:, :, there] - vel[:, 0:rows, there] * adjoint
                base[:, :, there] = jnp.clip(update, speed_floor, speed_ceiling)
                pltpu.make_async_copy(base.at[:, :, there], vel_out.at[:, :, there], out_sem.at[1 + n]).start()
            else:
                acc[:, there] = total
            return 0

        lax.fori_loop(0, blocks, one, 0)

    rows_in(0)
    weigh(0)
    for i in range(1, ny):
        r_copy(0, i).start()

    prow_copy.wait()
    player_copy.wait()

    def diverge(half_range):
        for l in range(layers):
            def div_rows(i, _, l=l):
                off = pl.multiple_of(i * 8, 8)
                here = pl.ds(off, 8)
                previous = dual[0, l, pl.ds(pl.multiple_of(jnp.maximum(off - 8, 0), 8), 8), :][7:8]
                outer = jnp.where(me == 0, 0.0, precv[l : l + 1, :])
                leading = jnp.where(i == 0, outer, previous)
                p0, p1, p2 = dual[0, l, here, :], dual[1, l, here, :], dual[2, l, here, :]
                prev_row = jnp.where(row8 == 0, leading, pltpu.roll(p0, 1, 0))
                prev_col = jnp.where(col8 == 0, 0.0, pltpu.roll(p1, 1, 1))
                if l > 0:
                    prev_layer = dual[2, l - 1, here, :]
                else:
                    prev_layer = jnp.where(my_depth == 0, 0.0, layer_prev[here, :])
                divergence = (p0 - prev_row) + (p1 - prev_col) + (p2 - prev_layer)
                v = vel[l, here, :]
                base[l, here, :] = v + primal_step * divergence
                root = lax.rsqrt(v)
                vel[l, here, :] = (primal_step * 0.25 * gardner_coef) * (root * jnp.sqrt(root))
                return 0

            lax.fori_loop(0, rows // 8, div_rows, 0)

    reduce_rows(0)
    diverge(None)
    spread(0)
    rows_out(0)

    rows_in(1)
    weigh(1)
    for i in range(1, ny):
        r_copy(1, i).start()
    reduce_rows(1)
    spread(1)
    rows_out(1)
    columns_back(0, False)
    columns_back(1, True)

    def ended(t, _):
        g_copy(1, t, me).wait_send()
        b_copy(0, t, me).wait_send()
        b_copy(1, t, me).wait_send()
        return 0

    lax.fori_loop(1, planes, ended, 0)
    for k in range(chunks):
        z_copy(k).wait_send()
        for i in range(1, ny):
            r_copy(k, i).wait_send()
            m_copy(k, i).wait_send()
    dual_store.wait()

    def stored(n, _):
        there = pl.ds(pl.multiple_of(n * block, block), block)
        pltpu.make_async_copy(base.at[:, :, there], vel_out.at[:, :, there], out_sem.at[1 + n]).wait()
        return 0

    lax.fori_loop(0, blocks, stored, 0)


def body(velocity, dual_field, kernel, data_spec, high, low):
    planes = lax.axis_size("plane")
    depths = lax.axis_size("depth")
    layers, rows, size = velocity.shape
    span = rows // chunks
    half = span // 2
    ny = depths // 2
    quarter = span // ny
    hbm = pl.BlockSpec(memory_space=pltpu.HBM)
    vmem = pltpu.VMEM
    dma = pltpu.SemaphoreType.DMA
    scratch = [
        vmem((layers, rows + 8, size), f32),
        vmem((3, layers, rows, size), f32),
        vmem((layers, rows, size), f32),
        vmem((rows, size), f32),
        vmem((planes, 2 * chunks, half, size), bf16),
        vmem((planes, 2 * chunks, half, size), bf16),
        vmem((size, 256), bf16),
        vmem((size, 256), bf16),
        vmem((size, 256), bf16),
        vmem((size, 256), bf16),
        vmem((chunks, planes, half, 384), f32),
        vmem((chunks, planes, half, 384), f32),
        vmem((chunks, planes, layers * half, 128), f32),
        vmem((chunks, planes, layers * half, 128), f32),
        vmem((2 * layers * span, size), bf16),
        vmem((chunks, span, size), f32),
        vmem((chunks, quarter, size), f32),
        vmem((chunks, ny, quarter, size), f32),
        vmem((chunks, quarter, size), f32),
        vmem((chunks, span, size), f32),
        vmem((2 * layers * rows, 2 * planes * half), bf16),
        vmem((layers * rows, size), f32),
        vmem((layers, rows, size), f32),
        vmem((8, size), f32),
        vmem((8, size), f32),
        vmem((8, size), f32),
        vmem((8, size), f32),
        vmem((rows, size), f32),
        vmem((rows, size), f32),
        dma((4,)),
        dma((2, 2 * chunks)),
        dma((1 + size // block,)),
        dma((chunks, planes)),
        dma((chunks, planes)),
        dma((chunks, planes)),
        dma((chunks, planes)),
        dma((chunks, ny)),
        dma((chunks, ny)),
        dma((2, chunks)),
        dma((chunks, ny)),
        dma((chunks, ny)),
        dma((8,)),
    ]
    return pl.pallas_call(
        functools.partial(step_kernel, planes, depths, size, layers),
        out_shape=(
            jax.ShapeDtypeStruct(velocity.shape, f32),
            jax.ShapeDtypeStruct(dual_field.shape, f32),
        ),
        in_specs=[hbm] * 6,
        out_specs=(hbm, hbm),
        scratch_shapes=scratch,
        compiler_params=pltpu.CompilerParams(
            collective_id=0, has_side_effects=True, vmem_limit_bytes=60 * 1024 * 1024
        ),
        cost_estimate=pl.CostEstimate(
            flops=24 * layers * rows * size * size, bytes_accessed=60 * layers * rows * size, transcendentals=layers * rows * size
        ),
    )(velocity, dual_field, kernel, data_spec, high, low)


def solution(mesh):
    in_specs = (
        P("depth", "plane", None),
        P(None, "depth", "plane", None),
        P("depth", "plane", None),
        P("plane", None),
        P(),
        P(),
    )
    out_specs = (P("depth", "plane", None), P(None, "depth", "plane", None))
    mapped = jax.shard_map(body, mesh=mesh, in_specs=in_specs, out_specs=out_specs, check_vma=False)

    def run(velocity, dual_field, kernel, data_spec):
        size, planes = velocity.shape[-1], mesh.shape["plane"]
        shape = (planes, 2 * chunks, size // planes // (2 * chunks), size)
        high, low = (part.reshape(shape) for part in cas_parts(size))
        return mapped(velocity, dual_field, kernel, data_spec, jnp.asarray(high), jnp.asarray(low))

    return run
```

time: 581 us -> 143 us (0.25)
  the two profiles are of different devices: /device:TPU:6 before, /device:TPU:1 now
where the time goes in v1:
time: 143 us; the launch traced here: 142 us
  Pallas kernels  134 us (94%)
  local copies, waits for them, and re-layouts  7.79 us (5%)
    pallas_call x1, Pallas kernels, body(): pl.pallas_call(functools.partial(step_kernel, planes, depths, size, layer...  134 us
    unnamed x2, local copies, waits for them, and re-layouts  7.79 us

profile of v1, /device:TPU:1, one launch (start us, length us, event | category | flops | bytes accessed | tf_op | source)
XLA Modules:
  0.0 142.4 jit_solution(3539649745840189952)
XLA Ops:
  0.6 134.0 %shard_map.77 = (f32[3,64,2048]{2,1,0:T(8,128)}, f32[3,3,64,2048]{3,2,1,0:T(8,128)}) custom-call(f32[3,64,2048]{2,1,0:T(8,128)} %vel_in.1, f32[3,3,64,2048]{3,2,1,0:T(8,128)} %dual_in.1, f32[3,64,2048]{2,1,0:T(8,128)} %kern_in.1, f32[64,2048]{1,0:T(8,128)} %data_in.1, bf16[32,4,16,2048]{3,2,1,0:T(8,128)(2,1)} %constant.4.clone.ahi_in, ...), custom_call_target="tpu_custom_call" | custom-call | flops 19327352832 | bytes 23592960 | tf_op jit(solution)/shard_map/pallas_call | solution.py:550
  134.6 2.7 %copy.10 = f32[3,64,2048]{2,1,0:T(8,128)} copy(f32[3,64,2048]{2,1,0:T(8,128)} %get-tuple-element.4) | data formatting | bytes 3145728
  137.3 5.1 %copy.11 = f32[3,3,64,2048]{3,2,1,0:T(8,128)} copy(f32[3,3,64,2048]{3,2,1,0:T(8,128)} %get-tuple-element.5) | data formatting | bytes 9437184

commit v2 on v1

--- a/solution.py
+++ b/solution.py
@@ -44,11 +44,11 @@
 def step_kernel(
     planes, depths, size, layers,
     vel_in, dual_in, kern_in, data_in, ahi_in, alo_in,
-    vel_out, dual_out,
-    vel, dual, kern, data, ahi, alo, dt0h, dt0l, dt1h, dt1l,
-    gsend, grecv, bsend, brecv, lhs, part, rsum, rrecv, zrecv, misfit, xt, acc, base,
+    base, dual,
+    vel, kern, data, ahi, alo, dt0h, dt0l, dt1h, dt1l,
+    gsend, grecv, bsend, brecv, lhs, part, rsum, rrecv, zrecv, misfit, xt, acc, spec,
     hsend, hrecv, psend, precv, layer_next, layer_prev,
-    in_sem, a_sem, out_sem, gs_sem, gr_sem, bs_sem, br_sem, rs_sem, rr_sem, z_sem, ms_sem, mr_sem, h_sem,
+    in_sem, a_sem, gs_sem, gr_sem, bs_sem, br_sem, rs_sem, rr_sem, z_sem, ms_sem, mr_sem, h_sem,
 ):
     rows = size // planes
     span = rows // chunks
@@ -153,7 +153,6 @@
     layer_copy = pltpu.make_async_remote_copy(
         src_ref=vel_in.at[0], dst_ref=layer_next, send_sem=h_sem.at[2], recv_sem=h_sem.at[3],
         device_id={"depth": below}, device_id_type=MESH)
-    layer_copy.start()
 
     def g_copy(k, t, who):
         to = target(t)
@@ -200,97 +199,102 @@
             copy.wait()
     columns(1, False)
 
-    row8 = lax.broadcasted_iota(jnp.int32, (8, size), 0)
-    col8 = lax.broadcasted_iota(jnp.int32, (8, size), 1)
-    loads[1].wait()
-    row_copy.wait()
-    layer_copy.wait()
-    for l in range(layers):
-        vel[l, rows : rows + 1, :] = hrecv[l : l + 1, :]
-
-    for l in range(layers):
-        def dual_rows(i, _, l=l):
-            off = pl.multiple_of(i * 8, 8)
-            here = pl.ds(off, 8)
-            v = vel[l, here, :]
-            following = vel[l, pl.ds(pl.multiple_of(off + 8, 8), 8), :][0:1]
-            next_row = jnp.where(row8 == 7, following, pltpu.roll(v, 7, 0))
-            next_col = pltpu.roll(v, size - 1, 1)
-            next_layer = vel[l + 1, here, :] if l + 1 < layers else layer_next[here, :]
-            last_row = (me * rows + off + row8) == size - 1
-            q0 = jnp.where(last_row, 0.0, dual[0, l, here, :] + dual_step * (next_row - v))
-            q1 = jnp.where(col8 == size - 1, 0.0, dual[1, l, here, :] + dual_step * (next_col - v))
-            q2 = dual[2, l, here, :] + dual_step * (next_layer - v)
-            if l + 1 == layers:
-                q2 = jnp.where(my_depth == depths - 1, 0.0, q2)
-            scale = lax.rsqrt(jnp.maximum(1.0, (q0 * q0 + q1 * q1 + q2 * q2) * (1.0 / (tv_weight * tv_weight))))
-            dual[0, l, here, :] = q0 * scale
-            dual[1, l, here, :] = q1 * scale
-            dual[2, l, here, :] = q2 * scale
-            return 0
-
-        lax.fori_loop(0, rows // 8, dual_rows, 0)
-    for l in range(layers):
-        psend[l : l + 1, :] = dual[0, l, rows - 1 : rows, :]
-    for l in range(layers, 8):
-        psend[l : l + 1, :] = jnp.zeros((1, size), f32)
-    dual_store = pltpu.make_async_copy(dual, dual_out, out_sem.at[0])
-    dual_store.start()
-    prow_copy = pltpu.make_async_remote_copy(
-        src_ref=psend, dst_ref=precv, send_sem=h_sem.at[4], recv_sem=h_sem.at[5],
-        device_id={"plane": after}, device_id_type=MESH)
-    prow_copy.start()
-    player_copy = pltpu.make_async_remote_copy(
-        src_ref=dual.at[2, layers - 1], dst_ref=layer_prev, send_sem=h_sem.at[6], recv_sem=h_sem.at[7],
-        device_id={"depth": above}, device_id_type=MESH)
-    player_copy.start()
-
-    def g_next(t, _):
-        g_copy(0, t, me).wait_send()
-        g_copy(1, t, me).start()
-        return 0
-
-    lax.fori_loop(1, planes, g_next, 0)
     loads[2].wait()
     loads[3].wait()
 
-    def rows_in(k):
-        def arrived(t, _):
-            g_copy(k, t, target(t)).wait_recv()
-            return 0
-
-        lax.fori_loop(1, planes, arrived, 0)
-
-        def assemble(m, _):
-            even, odd = grecv[k, 2 * m], grecv[k, 2 * m + 1]
-            a, b, c = (even[:, 0:128], odd[:, 0:128]), (even[:, 128:256], odd[:, 128:256]), (even[:, 256:384], odd[:, 256:384])
-            first = lambda p: jnp.where(left, p[0], swap(p[1]))
-            second = lambda p: jnp.where(left, swap(p[0]), p[1])
-            whole = jnp.concatenate([first(a), first(b), second(a), second(b), first(c), second(c)], axis=0)
-            high, low = split(whole)
-            there = pl.ds(pl.multiple_of(m * 128, 128), 128)
-            lhs[0 : layers * span, there] = high
-            lhs[layers * span : 2 * layers * span, there] = low
-            return 0
-
-        lax.fori_loop(0, planes // 2, assemble, 0)
+    groups = planes // group
+    wide = group * rows
+
+    def g_arrival(k, t, who):
+        return pltpu.make_async_remote_copy(
+            src_ref=gsend.at[k, who], dst_ref=grecv.at[k, who], send_sem=gs_sem.at[k, who], recv_sem=gr_sem.at[k, who],
+            device_id={"plane": who}, device_id_type=MESH)
+
+    def b_arrival(k, t, who):
+        return pltpu.make_async_remote_copy(
+            src_ref=bsend.at[k, who], dst_ref=brecv.at[k, who], send_sem=bs_sem.at[k, who], recv_sem=br_sem.at[k, who],
+            device_id={"plane": who}, device_id_type=MESH)
+
+    def source_group(g):
+        return (home + groups - g) % groups
+
+    def sources(g, arrival, k):
+        owner = source_group(g)
+
+        def arrived(i, _):
+            arrival(k, 0, owner * group + (seat + i) % group).wait_recv()
+            return 0
+
+        lax.fori_loop(jnp.where(g == 0, 1, 0), group, arrived, 0)
+
+    def g_start(k, g):
+        def start(t, _):
+            g_copy(k, t, me).start()
+            return 0
+
+        lax.fori_loop(max(g * group, 1), (g + 1) * group, start, 0)
+
+    def b_start(k, first, last):
+        def start(t, _):
+            b_copy(k, t, me).start()
+            return 0
+
+        lax.fori_loop(first, last, start, 0)
+
+    count = layers * span
+
+    def group_planes(g):
+        return pl.ds(pl.multiple_of(source_group(g) * group, group), group)
+
+    def rows_in(k, some, then=()):
+        for g in some:
+            sources(g, g_arrival, k)
+            if g < len(then) and then[g] is not None:
+                g_start(1, then[g])
+
+            def assemble(i, _, g=g):
+                m = source_group(g) * (group // 2) + i
+                even, odd = grecv[k, 2 * m], grecv[k, 2 * m + 1]
+                a, b, c = (even[:, 0:128], odd[:, 0:128]), (even[:, 128:256], odd[:, 128:256]), (even[:, 256:384], odd[:, 256:384])
+                first = lambda p: jnp.where(left, p[0], swap(p[1]))
+                second = lambda p: jnp.where(left, swap(p[0]), p[1])
+                whole = jnp.concatenate([first(a), first(b), second(a), second(b), first(c), second(c)], axis=0)
+                high, low = split(whole)
+                there = pl.ds(pl.multiple_of(g * wide + i * 128, 128), 128)
+                lhs[0:count, there] = high
+                lhs[count : 2 * count, there] = low
+                return 0
+
+            lax.fori_loop(0, group // 2, assemble, 0)
+        last = some[-1] + 1 == groups
+
+        def one(n, _):
+            there = pl.ds(pl.multiple_of(n * block, block), block)
+            spectra = spec[:, there] if some[0] > 0 else None
+            for g in some:
+                a_h = ahi[group_planes(g), :, :, there].reshape(wide, block)
+                a_l = alo[group_planes(g), :, :, there].reshape(wide, block)
+                both = dot(lhs[:, g * wide : (g + 1) * wide], a_h)
+                new = both[:count] + both[count:] + dot(lhs[0:count, g * wide : (g + 1) * wide], a_l)
+                spectra = new if spectra is None else spectra + new
+            if last:
+                weights = kern[:, k * span : (k + 1) * span, there]
+                part[k, :, there] = jnp.sum(weights * spectra.reshape(layers, span, block), axis=0)
+            else:
+                spec[:, there] = spectra
+            return 0
+
+        lax.fori_loop(0, blocks, one, 0)
+        if last:
+            for i in range(1, ny):
+                r_copy(k, i).start()
 
     def times_matrix(n):
         there = pl.ds(pl.multiple_of(n * block, block), block)
         a_h = ahi[:, :, :, there].reshape(size, block)
         a_l = alo[:, :, :, there].reshape(size, block)
-        count = layers * span
         both = dot(lhs[...], a_h)
-        return there, both[:count] + both[count:] + dot(lhs[0:count, :], a_l)
-
-    def weigh(k):
-        def one(n, _):
-            there, spectra = times_matrix(n)
-            weights = kern[:, k * span : (k + 1) * span, there]
-            part[k, :, there] = jnp.sum(weights * spectra.reshape(layers, span, block), axis=0)
-            return 0
-
-        lax.fori_loop(0, blocks, one, 0)
+        return both[:count] + both[count:] + dot(lhs[0:count, :], a_l)
 
     def r_copy(k, i):
         to = (y + i) % ny
@@ -338,10 +342,9 @@
         for i in range(1, ny):
             m_copy(k, i).start()
 
-    def rows_out(k):
+    def weigh_misfit(k):
         for i in range(1, ny):
             m_arrival(k, i).wait_recv()
-        count = layers * span
 
         def load(n, _):
             there = pl.ds(pl.multiple_of(n * block, block), block)
@@ -352,11 +355,13 @@
             return 0
 
         lax.fori_loop(0, blocks, load, 0)
-        left_all = lax.broadcasted_iota(jnp.int32, (layers, half, 128), 2) < 64
-
+
+    left_all = lax.broadcasted_iota(jnp.int32, (layers, half, 128), 2) < 64
+
+    def rows_out(k, begin, end):
         def one(i, _):
             n = (home * (group // per_block) + i) % blocks
-            _, values = times_matrix(n)
+            values = times_matrix(n)
             for s in range(block // 128):
                 slab = values[:, s * 128 : (s + 1) * 128].reshape(layers, 2, half, 128)
                 top, low = slab[:, 0], slab[:, 1]
@@ -368,70 +373,95 @@
             @pl.when(i % (group // per_block) == group // per_block - 1)
             def _():
                 g = i // (group // per_block)
-
-                def start(t, _):
-                    b_copy(k, t, me).start()
-                    return 0
-
-                lax.fori_loop(jnp.maximum(g * group, 1), (g + 1) * group, start, 0)
-
-            return 0
-
-        lax.fori_loop(0, blocks, one, 0)
-        brecv[k, me] = bsend[k, me]
-
-    def columns_back(k, last):
-        def arrived(t, _):
-            b_copy(k, t, target(t)).wait_recv()
-            return 0
-
-        lax.fori_loop(1, planes, arrived, 0)
-        high_rows = layers * rows
-        many = 128 // half
-
-        for l in range(layers):
-            def turn(i, _, l=l):
-                who = pl.ds(pl.multiple_of(i * many, many), many)
-                tile = brecv[k, who, l * half : (l + 1) * half, :].reshape(128, 128).T
+                b_start(k, jnp.maximum(g * group, 1), (g + 1) * group)
+
+            return 0
+
+        lax.fori_loop(begin, end, one, 0)
+        if begin == 0:
+            brecv[k, me] = bsend[k, me]
+
+    high_rows = layers * rows
+    tile_rows = group * half
+
+    def columns_back(k, some):
+        for g in some:
+            sources(g, b_arrival, k)
+            for l in range(layers):
+                tile = brecv[k, group_planes(g), l * half : (l + 1) * half, :].reshape(tile_rows, 128).T
                 high, low = split(tile)
                 for h in range(2):
-                    there = pl.ds(pl.multiple_of(h * planes * half + i * 128, 128), 128)
+                    there = pl.ds((2 * g + h) * tile_rows, tile_rows)
                     xt[l * rows : (l + 1) * rows, there] = high[h * 64 : (h + 1) * 64]
                     xt[high_rows + l * rows : high_rows + (l + 1) * rows, there] = low[h * 64 : (h + 1) * 64]
-                return 0
-
-            lax.fori_loop(0, planes // many, turn, 0)
+        first, final = k == 0 and some[0] == 0, k + 1 == chunks and some[-1] + 1 == groups
 
         def one(n, _):
             there = pl.ds(pl.multiple_of(n * block, block), block)
-            total = acc[:, there] if last else None
-            for h in range(2):
-                a_h = ahi[:, 2 * k + h, :, there].reshape(planes * half, block)
-                a_l = alo[:, 2 * k + h, :, there].reshape(planes * half, block)
-                part_x = xt[:, h * planes * half : (h + 1) * planes * half]
-                both = dot(part_x, a_h)
-                new = both[:high_rows] + both[high_rows:] + dot(part_x[:high_rows], a_l)
+            total = None if first else acc[:, there]
+            for g in some:
+                a_h = jnp.concatenate([ahi[group_planes(g), 2 * k + h, :, there].reshape(tile_rows, block) for h in range(2)], axis=0)
+                a_l = jnp.concatenate([alo[group_planes(g), 2 * k + h, :, there].reshape(tile_rows, block) for h in range(2)], axis=0)
+                where = pl.ds(2 * g * tile_rows, 2 * tile_rows)
+                both = dot(xt[:, where], a_h)
+                new = both[:high_rows] + both[high_rows:] + dot(xt[0:high_rows, where], a_l)
                 total = new if total is None else total + new
-            if last:
+            if final:
                 adjoint = total.reshape(layers, rows, block)
                 update = base[:, :, there] - vel[:, 0:rows, there] * adjoint
                 base[:, :, there] = jnp.clip(update, speed_floor, speed_ceiling)
-                pltpu.make_async_copy(base.at[:, :, there], vel_out.at[:, :, there], out_sem.at[1 + n]).start()
             else:
                 acc[:, there] = total
             return 0
 
         lax.fori_loop(0, blocks, one, 0)
 
-    rows_in(0)
-    weigh(0)
-    for i in range(1, ny):
-        r_copy(0, i).start()
-
-    prow_copy.wait()
-    player_copy.wait()
-
-    def diverge(half_range):
+    prow_copy = pltpu.make_async_remote_copy(
+        src_ref=psend, dst_ref=precv, send_sem=h_sem.at[4], recv_sem=h_sem.at[5],
+        device_id={"plane": after}, device_id_type=MESH)
+    player_copy = pltpu.make_async_remote_copy(
+        src_ref=dual.at[2, layers - 1], dst_ref=layer_prev, send_sem=h_sem.at[6], recv_sem=h_sem.at[7],
+        device_id={"depth": above}, device_id_type=MESH)
+
+    row8 = lax.broadcasted_iota(jnp.int32, (8, size), 0)
+    col8 = lax.broadcasted_iota(jnp.int32, (8, size), 1)
+
+    def update_dual():
+        loads[1].wait()
+        row_copy.wait()
+        layer_copy.wait()
+        for l in range(layers):
+            vel[l, rows : rows + 1, :] = hrecv[l : l + 1, :]
+
+        for l in range(layers):
+            def dual_rows(i, _, l=l):
+                off = pl.multiple_of(i * 8, 8)
+                here = pl.ds(off, 8)
+                v = vel[l, here, :]
+                following = vel[l, pl.ds(pl.multiple_of(off + 8, 8), 8), :][0:1]
+                next_row = jnp.where(row8 == 7, following, pltpu.roll(v, 7, 0))
+                next_col = pltpu.roll(v, size - 1, 1)
+                next_layer = vel[l + 1, here, :] if l + 1 < layers else layer_next[here, :]
+                last_row = (me * rows + off + row8) == size - 1
+                q0 = jnp.where(last_row, 0.0, dual[0, l, here, :] + dual_step * (next_row - v))
+                q1 = jnp.where(col8 == size - 1, 0.0, dual[1, l, here, :] + dual_step * (next_col - v))
+                q2 = dual[2, l, here, :] + dual_step * (next_layer - v)
+                if l + 1 == layers:
+                    q2 = jnp.where(my_depth == depths - 1, 0.0, q2)
+                scale = lax.rsqrt(jnp.maximum(1.0, (q0 * q0 + q1 * q1 + q2 * q2) * (1.0 / (tv_weight * tv_weight))))
+                dual[0, l, here, :] = q0 * scale
+                dual[1, l, here, :] = q1 * scale
+                dual[2, l, here, :] = q2 * scale
+                return 0
+
+            lax.fori_loop(0, rows // 8, dual_rows, 0)
+        for l in range(layers):
+            psend[l : l + 1, :] = dual[0, l, rows - 1 : rows, :]
+        for l in range(layers, 8):
+            psend[l : l + 1, :] = jnp.zeros((1, size), f32)
+    def diverge():
+        prow_copy.wait()
+        player_copy.wait()
         for l in range(layers):
             def div_rows(i, _, l=l):
                 off = pl.multiple_of(i * 8, 8)
@@ -455,22 +485,32 @@
 
             lax.fori_loop(0, rows // 8, div_rows, 0)
 
+    early, late = tuple(range(groups - 1)), (groups - 1,)
+    rows_in(0, early, (0, 1))
+    rows_in(0, late, (None,) * (groups - 1) + (2,))
     reduce_rows(0)
-    diverge(None)
+    g_start(1, 3)
+    layer_copy.start()
+    rows_in(1, early)
     spread(0)
-    rows_out(0)
-
-    rows_in(1)
-    weigh(1)
-    for i in range(1, ny):
-        r_copy(1, i).start()
+    rows_in(1, late)
+    weigh_misfit(0)
+    rows_out(0, 0, blocks // 2)
     reduce_rows(1)
+    rows_out(0, blocks // 2, blocks)
+    update_dual()
+    prow_copy.start()
+    player_copy.start()
     spread(1)
-    rows_out(1)
-    columns_back(0, False)
-    columns_back(1, True)
+    weigh_misfit(1)
+    rows_out(1, 0, blocks)
+    columns_back(0, early + late)
+    diverge()
+    columns_back(1, early)
+    columns_back(1, late)
 
     def ended(t, _):
+        g_copy(0, t, me).wait_send()
         g_copy(1, t, me).wait_send()
         b_copy(0, t, me).wait_send()
         b_copy(1, t, me).wait_send()
@@ -482,14 +522,15 @@
         for i in range(1, ny):
             r_copy(k, i).wait_send()
             m_copy(k, i).wait_send()
-    dual_store.wait()
-
-    def stored(n, _):
-        there = pl.ds(pl.multiple_of(n * block, block), block)
-        pltpu.make_async_copy(base.at[:, :, there], vel_out.at[:, :, there], out_sem.at[1 + n]).wait()
-        return 0
-
-    lax.fori_loop(0, blocks, stored, 0)
+
+
+def store_kernel(vel, dual, vel_out, dual_out, sem):
+    copies = [pltpu.make_async_copy(dual.at[c], dual_out.at[c], sem.at[c]) for c in range(3)]
+    copies.append(pltpu.make_async_copy(vel, vel_out, sem.at[3]))
+    for copy in copies:
+        copy.start()
+    for copy in copies:
+        copy.wait()
 
 
 def body(velocity, dual_field, kernel, data_spec, high, low):
@@ -505,7 +546,6 @@
     dma = pltpu.SemaphoreType.DMA
     scratch = [
         vmem((layers, rows + 8, size), f32),
-        vmem((3, layers, rows, size), f32),
         vmem((layers, rows, size), f32),
         vmem((rows, size), f32),
         vmem((planes, 2 * chunks, half, size), bf16),
@@ -526,7 +566,7 @@
         vmem((chunks, span, size), f32),
         vmem((2 * layers * rows, 2 * planes * half), bf16),
         vmem((layers * rows, size), f32),
-        vmem((layers, rows, size), f32),
+        vmem((layers * span, size), f32),
         vmem((8, size), f32),
         vmem((8, size), f32),
         vmem((8, size), f32),
@@ -535,7 +575,6 @@
         vmem((rows, size), f32),
         dma((4,)),
         dma((2, 2 * chunks)),
-        dma((1 + size // block,)),
         dma((chunks, planes)),
         dma((chunks, planes)),
         dma((chunks, planes)),
@@ -547,22 +586,31 @@
         dma((chunks, ny)),
         dma((8,)),
     ]
-    return pl.pallas_call(
+    on_chip = pl.BlockSpec(memory_space=vmem)
+    updated = pl.pallas_call(
         functools.partial(step_kernel, planes, depths, size, layers),
-        out_shape=(
-            jax.ShapeDtypeStruct(velocity.shape, f32),
-            jax.ShapeDtypeStruct(dual_field.shape, f32),
-        ),
+        out_shape=(vmem(velocity.shape, f32), vmem(dual_field.shape, f32)),
         in_specs=[hbm] * 6,
-        out_specs=(hbm, hbm),
+        out_specs=(on_chip, on_chip),
         scratch_shapes=scratch,
         compiler_params=pltpu.CompilerParams(
-            collective_id=0, has_side_effects=True, vmem_limit_bytes=60 * 1024 * 1024
+            collective_id=0, has_side_effects=True, vmem_limit_bytes=48 * 1024 * 1024
         ),
         cost_estimate=pl.CostEstimate(
             flops=24 * layers * rows * size * size, bytes_accessed=60 * layers * rows * size, transcendentals=layers * rows * size
         ),
     )(velocity, dual_field, kernel, data_spec, high, low)
+    return pl.pallas_call(
+        store_kernel,
+        out_shape=(
+            jax.ShapeDtypeStruct(velocity.shape, f32),
+            jax.ShapeDtypeStruct(dual_field.shape, f32),
+        ),
+        in_specs=[on_chip, on_chip],
+        out_specs=(hbm, hbm),
+        scratch_shapes=[dma((4,))],
+        compiler_params=pltpu.CompilerParams(has_side_effects=True, vmem_limit_bytes=8 * 1024 * 1024),
+    )(*updated)
 
 
 def solution(mesh):

time: 143 us -> 124 us (0.87)
  Pallas kernels: 134 us -> 123 us
  local copies, waits for them, and re-layouts: 7.79 us -> 0 us
    pallas_call x1, Pallas kernels: 134 us -> 120 us  [body(): pl.pallas_call(functools.partial(step_kernel, planes, depths, size, layer...]
    unnamed x2 -> x0, local copies, waits for them, and re-layouts: 7.79 us -> none
    pallas_call x0 -> x1, Pallas kernels: none -> 2.73 us  [body(): pl.pallas_call(store_kernel, out_shape=(jax.ShapeDtypeStruct(velocity.sha...]
where the time goes in v2:
time: 124 us; the launch traced here: 123 us
  Pallas kernels  123 us (99%)
    pallas_call x1, Pallas kernels, body(): pl.pallas_call(functools.partial(step_kernel, planes, depths, size, layer...  120 us
    pallas_call x1, Pallas kernels, body(): pl.pallas_call(store_kernel, out_shape=(jax.ShapeDtypeStruct(velocity.sha...  2.73 us

profile of v2, /device:TPU:1, one launch (start us, length us, event | category | flops | bytes accessed | tf_op | source)
XLA Modules:
  0.0 123.3 jit_solution(2090838076723368480)
XLA Ops:
  0.6 119.9 %shard_map.77 = (f32[3,64,2048]{2,1,0:T(8,128)S(1)}, f32[3,3,64,2048]{3,2,1,0:T(8,128)S(1)}) custom-call(f32[3,64,2048]{2,1,0:T(8,128)} %vel_in.1, f32[3,3,64,2048]{3,2,1,0:T(8,128)} %dual_in.1, f32[3,64,2048]{2,1,0:T(8,128)} %kern_in.1, f32[64,2048]{1,0:T(8,128)} %data_in.1, bf16[32,4,16,2048]{3,2,1,0:T(8,128)(2,1)} %constant.4.clone.ahi_in, ...), custom_call_target="tpu_custom_call" | custom-call | flops 19327352832 | bytes 23592960 | tf_op jit(solution)/shard_map/pallas_call | solution.py:590
  120.6 2.7 %shard_map.78 = (f32[3,64,2048]{2,1,0:T(8,128)}, f32[3,3,64,2048]{3,2,1,0:T(8,128)}) custom-call(f32[3,64,2048]{2,1,0:T(8,128)S(1)} %get-tuple-element.4.vel, f32[3,3,64,2048]{3,2,1,0:T(8,128)S(1)} %get-tuple-element.5.dual), custom_call_target="tpu_custom_call" | custom-call | tf_op jit(solution)/shard_map/pallas_call | solution.py:603

commit v3 on v2

--- a/solution.py
+++ b/solution.py
@@ -144,12 +144,9 @@
     for l in range(layers, 8):
         hsend[l : l + 1, :] = jnp.zeros((1, size), f32)
 
-    pl.semaphore_wait(barrier, planes + ny)
-
     row_copy = pltpu.make_async_remote_copy(
         src_ref=hsend, dst_ref=hrecv, send_sem=h_sem.at[0], recv_sem=h_sem.at[1],
         device_id={"plane": before}, device_id_type=MESH)
-    row_copy.start()
     layer_copy = pltpu.make_async_remote_copy(
         src_ref=vel_in.at[0], dst_ref=layer_next, send_sem=h_sem.at[2], recv_sem=h_sem.at[3],
         device_id={"depth": below}, device_id_type=MESH)
@@ -166,7 +163,14 @@
             src_ref=bsend.at[k, to], dst_ref=brecv.at[k, who], send_sem=bs_sem.at[k, to], recv_sem=br_sem.at[k, who],
             device_id={"plane": to}, device_id_type=MESH)
 
-    def columns(k, send):
+    def g_start(k, g):
+        def start(t, _):
+            g_copy(k, t, me).start()
+            return 0
+
+        lax.fori_loop(max(g * group, 1), (g + 1) * group, start, 0)
+
+    def columns(k, send, begin, end):
         def one(g, _):
             first = pl.multiple_of(((home + g) % (planes // group)) * group, group)
             there = pl.ds(first, group)
@@ -187,17 +191,22 @@
                 lax.fori_loop(jnp.maximum(g * group, 1), (g + 1) * group, start, 0)
             return 0
 
-        lax.fori_loop(0, planes // group, one, 0)
-        grecv[k, me] = gsend[k, me]
+        lax.fori_loop(begin, end, one, 0)
+        if begin == 0:
+            grecv[k, me] = gsend[k, me]
 
     for pair in a_loads[:2]:
         for copy in pair:
             copy.wait()
-    columns(0, True)
+    columns(0, False, 0, 1)
+    pl.semaphore_wait(barrier, planes + ny)
+    g_start(0, 0)
+    columns(0, True, 1, planes // group)
+    row_copy.start()
     for pair in a_loads[2:]:
         for copy in pair:
             copy.wait()
-    columns(1, False)
+    columns(1, False, 0, planes // group)
 
     loads[2].wait()
     loads[3].wait()
@@ -226,13 +235,6 @@
             return 0
 
         lax.fori_loop(jnp.where(g == 0, 1, 0), group, arrived, 0)
-
-    def g_start(k, g):
-        def start(t, _):
-            g_copy(k, t, me).start()
-            return 0
-
-        lax.fori_loop(max(g * group, 1), (g + 1) * group, start, 0)
 
     def b_start(k, first, last):
         def start(t, _):
@@ -394,7 +396,7 @@
                     there = pl.ds((2 * g + h) * tile_rows, tile_rows)
                     xt[l * rows : (l + 1) * rows, there] = high[h * 64 : (h + 1) * 64]
                     xt[high_rows + l * rows : high_rows + (l + 1) * rows, there] = low[h * 64 : (h + 1) * 64]
-        first, final = k == 0 and some[0] == 0, k + 1 == chunks and some[-1] + 1 == groups
+        first = k == 0 and some[0] == 0
 
         def one(n, _):
             there = pl.ds(pl.multiple_of(n * block, block), block)
@@ -406,12 +408,7 @@
                 both = dot(xt[:, where], a_h)
                 new = both[:high_rows] + both[high_rows:] + dot(xt[0:high_rows, where], a_l)
                 total = new if total is None else total + new
-            if final:
-                adjoint = total.reshape(layers, rows, block)
-                update = base[:, :, there] - vel[:, 0:rows, there] * adjoint
-                base[:, :, there] = jnp.clip(update, speed_floor, speed_ceiling)
-            else:
-                acc[:, there] = total
+            acc[:, there] = total
             return 0
 
         lax.fori_loop(0, blocks, one, 0)
@@ -419,9 +416,15 @@
     prow_copy = pltpu.make_async_remote_copy(
         src_ref=psend, dst_ref=precv, send_sem=h_sem.at[4], recv_sem=h_sem.at[5],
         device_id={"plane": after}, device_id_type=MESH)
-    player_copy = pltpu.make_async_remote_copy(
-        src_ref=dual.at[2, layers - 1], dst_ref=layer_prev, send_sem=h_sem.at[6], recv_sem=h_sem.at[7],
-        device_id={"depth": above}, device_id_type=MESH)
+    part_rows = rows // 2
+    player_copies = [
+        pltpu.make_async_remote_copy(
+            src_ref=dual.at[2, layers - 1, pl.ds(h * part_rows, part_rows)],
+            dst_ref=layer_prev.at[pl.ds(h * part_rows, part_rows)],
+            send_sem=h_sem.at[6 + 2 * h], recv_sem=h_sem.at[7 + 2 * h],
+            device_id={"depth": above}, device_id_type=MESH)
+        for h in range(2)
+    ]
 
     row8 = lax.broadcasted_iota(jnp.int32, (8, size), 0)
     col8 = lax.broadcasted_iota(jnp.int32, (8, size), 1)
@@ -459,10 +462,8 @@
             psend[l : l + 1, :] = dual[0, l, rows - 1 : rows, :]
         for l in range(layers, 8):
             psend[l : l + 1, :] = jnp.zeros((1, size), f32)
-    def diverge():
-        prow_copy.wait()
-        player_copy.wait()
-        for l in range(layers):
+    def diverge(some, begin, end):
+        for l in some:
             def div_rows(i, _, l=l):
                 off = pl.multiple_of(i * 8, 8)
                 here = pl.ds(off, 8)
@@ -483,13 +484,23 @@
                 vel[l, here, :] = (primal_step * 0.25 * gardner_coef) * (root * jnp.sqrt(root))
                 return 0
 
-            lax.fori_loop(0, rows // 8, div_rows, 0)
+            lax.fori_loop(begin, end, div_rows, 0)
 
     early, late = tuple(range(groups - 1)), (groups - 1,)
-    rows_in(0, early, (0, 1))
-    rows_in(0, late, (None,) * (groups - 1) + (2,))
+    def update_velocity(some, begin, end):
+        for l in some:
+            def new_rows(i, _, l=l):
+                here = pl.ds(pl.multiple_of(i * 8, 8), 8)
+                there = pl.ds(pl.multiple_of(l * rows + i * 8, 8), 8)
+                update = base[l, here, :] - vel[l, here, :] * acc[there, :]
+                base[l, here, :] = jnp.clip(update, speed_floor, speed_ceiling)
+                return 0
+
+            lax.fori_loop(begin, end, new_rows, 0)
+
+    rows_in(0, early, tuple(range(groups - 1)))
+    rows_in(0, late, (None,) * (groups - 1) + (groups - 1,))
     reduce_rows(0)
-    g_start(1, 3)
     layer_copy.start()
     rows_in(1, early)
     spread(0)
@@ -500,14 +511,23 @@
     rows_out(0, blocks // 2, blocks)
     update_dual()
     prow_copy.start()
-    player_copy.start()
     spread(1)
     weigh_misfit(1)
     rows_out(1, 0, blocks)
+    player_copies[0].start()
+    player_copies[1].start()
     columns_back(0, early + late)
-    diverge()
+    prow_copy.wait()
+    diverge(range(1, layers), 0, rows // 8)
     columns_back(1, early)
     columns_back(1, late)
+    update_velocity(range(1, layers), 0, rows // 8)
+    player_copies[0].wait()
+    diverge((0,), 0, rows // 16)
+    update_velocity((0,), 0, rows // 16)
+    player_copies[1].wait()
+    diverge((0,), rows // 16, rows // 8)
+    update_velocity((0,), rows // 16, rows // 8)
 
     def ended(t, _):
         g_copy(0, t, me).wait_send()
@@ -525,8 +545,11 @@
 
 
 def store_kernel(vel, dual, vel_out, dual_out, sem):
-    copies = [pltpu.make_async_copy(dual.at[c], dual_out.at[c], sem.at[c]) for c in range(3)]
-    copies.append(pltpu.make_async_copy(vel, vel_out, sem.at[3]))
+    layers = vel.shape[0]
+    copies = [
+        pltpu.make_async_copy(dual.at[c, l], dual_out.at[c, l], sem.at[c, l]) for c in range(3) for l in range(layers)
+    ]
+    copies += [pltpu.make_async_copy(vel.at[l], vel_out.at[l], sem.at[3, l]) for l in range(layers)]
     for copy in copies:
         copy.start()
     for copy in copies:
@@ -584,7 +607,7 @@
         dma((2, chunks)),
         dma((chunks, ny)),
         dma((chunks, ny)),
-        dma((8,)),
+        dma((10,)),
     ]
     on_chip = pl.BlockSpec(memory_space=vmem)
     updated = pl.pallas_call(
@@ -608,7 +631,7 @@
         ),
         in_specs=[on_chip, on_chip],
         out_specs=(hbm, hbm),
-        scratch_shapes=[dma((4,))],
+        scratch_shapes=[dma((4, layers))],
         compiler_params=pltpu.CompilerParams(has_side_effects=True, vmem_limit_bytes=8 * 1024 * 1024),
     )(*updated)
 

time: 124 us -> 119 us (0.960)
  Pallas kernels: 123 us -> 118 us
    pallas_call x1, Pallas kernels: 120 us -> 115 us  [body(): pl.pallas_call(functools.partial(step_kernel, planes, depths, size, layer...]
where the time goes in v3:
time: 119 us; the launch traced here: 118 us
  Pallas kernels  118 us (99%)
    pallas_call x1, Pallas kernels, body(): pl.pallas_call(functools.partial(step_kernel, planes, depths, size, layer...  115 us
    pallas_call x1, Pallas kernels, body(): pl.pallas_call(store_kernel, out_shape=(jax.ShapeDtypeStruct(velocity.sha...  2.75 us

profile of v3, /device:TPU:1, one launch (start us, length us, event | category | flops | bytes accessed | tf_op | source)
XLA Modules:
  0.0 118.3 jit_solution(7062492098590972405)
XLA Ops:
  0.6 114.9 %shard_map.77 = (f32[3,64,2048]{2,1,0:T(8,128)S(1)}, f32[3,3,64,2048]{3,2,1,0:T(8,128)S(1)}) custom-call(f32[3,64,2048]{2,1,0:T(8,128)} %vel_in.1, f32[3,3,64,2048]{3,2,1,0:T(8,128)} %dual_in.1, f32[3,64,2048]{2,1,0:T(8,128)} %kern_in.1, f32[64,2048]{1,0:T(8,128)} %data_in.1, bf16[32,4,16,2048]{3,2,1,0:T(8,128)(2,1)} %constant.4.clone.ahi_in, ...), custom_call_target="tpu_custom_call" | custom-call | flops 19327352832 | bytes 23592960 | tf_op jit(solution)/shard_map/pallas_call | solution.py:613
  115.5 2.8 %shard_map.78 = (f32[3,64,2048]{2,1,0:T(8,128)}, f32[3,3,64,2048]{3,2,1,0:T(8,128)}) custom-call(f32[3,64,2048]{2,1,0:T(8,128)S(1)} %get-tuple-element.4.vel, f32[3,3,64,2048]{3,2,1,0:T(8,128)S(1)} %get-tuple-element.5.dual), custom_call_target="tpu_custom_call" | custom-call | tf_op jit(solution)/shard_map/pallas_call | solution.py:626

commit v4 on v3

--- a/solution.py
+++ b/solution.py
@@ -506,12 +506,11 @@
     spread(0)
     rows_in(1, late)
     weigh_misfit(0)
-    rows_out(0, 0, blocks // 2)
     reduce_rows(1)
-    rows_out(0, blocks // 2, blocks)
+    rows_out(0, 0, blocks)
+    spread(1)
     update_dual()
     prow_copy.start()
-    spread(1)
     weigh_misfit(1)
     rows_out(1, 0, blocks)
     player_copies[0].start()

time: 119 us -> 120 us (level)
    pallas_call x1, Pallas kernels: 115 us -> 116 us  [body(): pl.pallas_call(functools.partial(step_kernel, planes, depths, size, layer...]
where the time goes in v4:
time: 120 us
  Pallas kernels  119 us (99%)
    pallas_call x1, Pallas kernels, body(): pl.pallas_call(functools.partial(step_kernel, planes, depths, size, layer...  116 us
    pallas_call x1, Pallas kernels, body(): pl.pallas_call(store_kernel, out_shape=(jax.ShapeDtypeStruct(velocity.sha...  2.75 us

profile of v4, /device:TPU:1, one launch (start us, length us, event | category | flops | bytes accessed | tf_op | source)
XLA Modules:
  0.0 119.6 jit_solution(17306897733220109692)
XLA Ops:
  0.6 116.2 %shard_map.77 = (f32[3,64,2048]{2,1,0:T(8,128)S(1)}, f32[3,3,64,2048]{3,2,1,0:T(8,128)S(1)}) custom-call(f32[3,64,2048]{2,1,0:T(8,128)} %vel_in.1, f32[3,3,64,2048]{3,2,1,0:T(8,128)} %dual_in.1, f32[3,64,2048]{2,1,0:T(8,128)} %kern_in.1, f32[64,2048]{1,0:T(8,128)} %data_in.1, bf16[32,4,16,2048]{3,2,1,0:T(8,128)(2,1)} %constant.4.clone.ahi_in, ...), custom_call_target="tpu_custom_call" | custom-call | flops 19327352832 | bytes 23592960 | tf_op jit(solution)/shard_map/pallas_call | solution.py:612
  116.8 2.8 %shard_map.78 = (f32[3,64,2048]{2,1,0:T(8,128)}, f32[3,3,64,2048]{3,2,1,0:T(8,128)}) custom-call(f32[3,64,2048]{2,1,0:T(8,128)S(1)} %get-tuple-element.4.vel, f32[3,3,64,2048]{3,2,1,0:T(8,128)S(1)} %get-tuple-element.5.dual), custom_call_target="tpu_custom_call" | custom-call | tf_op jit(solution)/shard_map/pallas_call | solution.py:625
